TPU v7x, 32 devices: a whole 2x2x4 slice. The times are simulated.
32 devices in a mesh: dp: 4 (over y, x), ctx: 8 (over z, core).
Axes of the slice: x: 2, y: 2, z: 4, core: 2. Of those that a mesh axis runs over, the one named last changes fastest.
Arguments:
- queries: bfloat16 [5120, 4096], P(('dp', 'ctx')), may hold values from -20 to 20
- keys: bfloat16 [5120, 512], P(('dp', 'ctx')), may hold values from -6 to 6
- values: bfloat16 [5120, 512], P(('dp', 'ctx')), may hold values from -6 to 6
- output_gradient: bfloat16 [5120, 4096], P(('dp', 'ctx')), may hold values from -24 to 24
- adapter_rank_cotangent: bfloat16 [5120, 32], P(('dp', 'ctx')), may hold values from -64 to 64
- adapter_down_weight: bfloat16 [4096, 32], replicated, may hold values from -0.09375 to 0.09375
- relay_owner_index: int32 [32, 64], P(('dp', 'ctx')), may hold values from 0 to 7, as said below
- relay_block_slot: int32 [32, 64], P(('dp', 'ctx')), may hold values from 0 to 63, as said below
- short_rollout_lengths: int32 [32, 4], P(('dp', 'ctx')), may hold values from 1 to 16, 32 in all within a row
Outputs:
- owner_query_gradient: bfloat16 [5120, 4096], P(('dp', 'ctx'))
- owner_key_gradient: bfloat16 [5120, 512], P(('dp', 'ctx'))
- owner_value_gradient: bfloat16 [5120, 512], P(('dp', 'ctx'))
- adapter_down_gradient: float32 [4096, 32], P(('dp', 'ctx'))
Inputs may be any that keep to these rules, and one draw needn't show every extreme that they name: `relay_owner_index`: blocks stay on their line (same data index). Every owner receives exactly 64 blocks, at most 12 from one device, and on every line some device sends exactly 12 blocks to one owner. On each line the pairs (relay_owner_index, relay_block_slot) are all different.
All inputs are finite; a program needn't handle non-finite values.
Results may differ from a plain program's by a relative error of at most 0.0093.
Values may be sent and summed in bfloat16 or wider, within the bound.
A program may use at most 128 MiB of HBM per device.

v0:
```python
import math

import jax
import jax.numpy as jnp
from jax import lax
from jax.experimental import pallas as pl
from jax.experimental.pallas import tpu as pltpu
from jax.sharding import PartitionSpec as P

HEAD_SIZE = 128
QUERY_HEADS = 32
KVH = 4
GROUP = 8
ADAPTER_RANK = 32
LONG_DEVICE_ROWS = 128
SHORT_DEV = 32
SUB = 4
BLK = 2
NB = 64
DEVICE_ROWS = 160


NEG_FILL = -1e30


def from_behind(shard, axis, by):
    count = lax.axis_size(axis)
    pairs = [(i, i + by) for i in range(count) if 0 <= i + by < count]
    return lax.ppermute(shard, axis, pairs)


def shifted(block, axis, distance):
    devices = range(lax.axis_size(axis))
    route = [((i - distance) % len(devices), i) for i in devices]
    return lax.ppermute(block, axis, route)


def head_scores(query4, key3):
    raw = jnp.einsum("ikgd,jkd->kgij", query4, key3, preferred_element_type=jnp.float32)
    return raw * (1.0 / math.sqrt(query4.shape[3]))


def running_stats(state, query4, key3, visible_mask):
    best, mass = state
    raw = head_scores(query4, key3)
    fresh = jnp.maximum(best, jnp.max(jnp.where(visible_mask, raw, NEG_FILL), axis=-1))
    mass = mass * jnp.exp(best - fresh) + jnp.sum(
        jnp.where(visible_mask, jnp.exp(raw - fresh[..., None]), 0.0), axis=-1
    )
    return (fresh, mass)


def block_weights(query4, key3, visible_mask, log_total):
    raw = head_scores(query4, key3)
    return jnp.where(visible_mask, jnp.exp(raw - log_total[..., None]), 0.0).astype(jnp.bfloat16)


def forward_values(attended, query4, key3, value3, visible_mask, log_total):
    weights = block_weights(query4, key3, visible_mask, log_total)
    return attended + jnp.einsum(
        "kgij,jkd->ikgd", weights, value3, preferred_element_type=jnp.float32
    )


def backward_block(query4, key3, value3, grad4, visible_mask, log_total, delta):
    weights = block_weights(query4, key3, visible_mask, log_total)
    dprob = jnp.einsum("ikgd,jkd->kgij", grad4, value3, preferred_element_type=jnp.float32)
    dscore = (
        weights.astype(jnp.float32)
        * (dprob - delta[..., None])
        * (1.0 / math.sqrt(query4.shape[3]))
    ).astype(jnp.bfloat16)
    part_q = jnp.einsum("kgij,jkd->ikgd", dscore, key3, preferred_element_type=jnp.float32)
    part_k = jnp.einsum("kgij,ikgd->jkd", dscore, query4, preferred_element_type=jnp.float32)
    part_v = jnp.einsum("kgij,ikgd->jkd", weights, grad4, preferred_element_type=jnp.float32)
    return (part_q, part_k, part_v)


def row_delta(grad4, attended):
    return jnp.einsum("ikgd,ikgd->kgi", grad4.astype(jnp.float32), attended)


def shards(
    queries,
    keys,
    values,
    output_gradient,
    adapter_rank_cotangent,
    adapter_down_weight,
    relay_owner_index,
    relay_block_slot,
    short_rollout_lengths,
):
    line_size = lax.axis_size("ctx")
    slots_each = 3 * NB // (2 * line_size)
    owners = relay_owner_index[0]
    targets = relay_block_slot[0]
    block_ids = jnp.arange(NB, dtype=jnp.int32)
    same_owner = owners[:, None] == owners[None, :]
    earlier = block_ids[None, :] < block_ids[:, None]
    within = jnp.sum((same_owner & earlier).astype(jnp.int32), axis=1)
    position = owners * slots_each + within
    buffer_ids = jnp.arange(line_size * slots_each, dtype=jnp.int32)
    matches = position[None, :] == buffer_ids[:, None]
    filled = jnp.any(matches, axis=1)
    source_ids = jnp.sum(jnp.where(matches, block_ids[None, :], 0), axis=1)
    carried = jnp.where(filled, jnp.sum(jnp.where(matches, targets[None, :], 0), axis=1), -1)

    def packed_rows(rows_in):
        blocks = rows_in[:LONG_DEVICE_ROWS].reshape(NB, BLK, rows_in.shape[1])
        chosen = jnp.take(blocks, source_ids, axis=0)
        return jnp.where(filled[:, None, None], chosen, jnp.zeros_like(chosen))

    arrived = (
        lax.all_to_all(packed_rows(queries), "ctx", split_axis=0, concat_axis=0, tiled=True),
        lax.all_to_all(packed_rows(keys), "ctx", split_axis=0, concat_axis=0, tiled=True),
        lax.all_to_all(packed_rows(values), "ctx", split_axis=0, concat_axis=0, tiled=True),
        lax.all_to_all(
            packed_rows(output_gradient), "ctx", split_axis=0, concat_axis=0, tiled=True
        ),
        lax.all_to_all(
            packed_rows(adapter_rank_cotangent), "ctx", split_axis=0, concat_axis=0, tiled=True
        ),
        lax.all_to_all(
            carried.astype(jnp.bfloat16), "ctx", split_axis=0, concat_axis=0, tiled=True
        ),
    )
    landing = arrived[5].astype(jnp.int32)
    pick_from = jnp.sum(
        jnp.where(landing[None, :] == block_ids[:, None], buffer_ids[None, :], 0), axis=1
    )

    def unpacked(received):
        return jnp.take(received, pick_from, axis=0).reshape(LONG_DEVICE_ROWS, received.shape[2])

    long_q = unpacked(arrived[0])
    long_k = unpacked(arrived[1])
    long_v = unpacked(arrived[2])
    long_d = unpacked(arrived[3])
    long_c = unpacked(arrived[4])

    def total_grad(output_cotangent, adapter_cotangent):
        branch_choice = jnp.einsum(
            "fe,ve->fv", adapter_cotangent, adapter_down_weight, preferred_element_type=jnp.float32
        )
        return (output_cotangent.astype(jnp.float32) + branch_choice).astype(jnp.bfloat16)

    short_q = queries[LONG_DEVICE_ROWS:].reshape(SHORT_DEV, KVH, GROUP, HEAD_SIZE)
    short_k = keys[LONG_DEVICE_ROWS:].reshape(SHORT_DEV, KVH, HEAD_SIZE)
    short_v = values[LONG_DEVICE_ROWS:].reshape(SHORT_DEV, KVH, HEAD_SIZE)
    short_cotangent = adapter_rank_cotangent[LONG_DEVICE_ROWS:]
    short_g = total_grad(output_gradient[LONG_DEVICE_ROWS:], short_cotangent).reshape(
        SHORT_DEV, KVH, GROUP, HEAD_SIZE
    )
    ends = jnp.cumsum(short_rollout_lengths[0])
    short_ids = jnp.arange(SHORT_DEV, dtype=jnp.int32)
    segment = jnp.sum((ends[None, :] <= short_ids[:, None]).astype(jnp.int32), axis=1)
    short_seen = (segment[:, None] == segment[None, :]) & (short_ids[None, :] <= short_ids[:, None])
    short_best = jnp.full((KVH, GROUP, SHORT_DEV), NEG_FILL, jnp.float32)
    short_best, short_mass = running_stats(
        (short_best, jnp.zeros_like(short_best)), short_q, short_k, short_seen
    )
    short_log = short_best + jnp.log(short_mass)
    short_att = forward_values(
        jnp.zeros((SHORT_DEV, KVH, GROUP, HEAD_SIZE), jnp.float32),
        short_q,
        short_k,
        short_v,
        short_seen,
        short_log,
    )
    short_delta = row_delta(short_g, short_att)
    short_dq, short_dk, short_dv = backward_block(
        short_q, short_k, short_v, short_g, short_seen, short_log, short_delta
    )
    query4 = long_q.reshape(LONG_DEVICE_ROWS, KVH, GROUP, HEAD_SIZE)
    key3 = long_k.reshape(LONG_DEVICE_ROWS, KVH, HEAD_SIZE)
    value3 = long_v.reshape(LONG_DEVICE_ROWS, KVH, HEAD_SIZE)
    grad4 = total_grad(long_d, long_c).reshape(LONG_DEVICE_ROWS, KVH, GROUP, HEAD_SIZE)
    member = lax.axis_index("ctx") % SUB
    row_ids = jnp.arange(LONG_DEVICE_ROWS, dtype=jnp.int32)

    def long_mask(hop_index):
        source = member - hop_index
        return (source >= 0) & (
            source * LONG_DEVICE_ROWS + row_ids[None, :]
            <= member * LONG_DEVICE_ROWS + row_ids[:, None]
        )

    best = jnp.full((KVH, GROUP, LONG_DEVICE_ROWS), NEG_FILL, jnp.float32)
    mass = jnp.zeros_like(best)
    stored = []
    key_now, value_now = (key3, value3)
    for hop_index in range(SUB):
        if hop_index > 0:
            key_now, value_now = from_behind((key_now, value_now), "ctx", 1)
        stored.append((key_now, value_now))
        best, mass = lax.cond(
            hop_index <= member,
            lambda state, kk=key_now, hh=hop_index: running_stats(state, query4, kk, long_mask(hh)),
            lambda state: state,
            (best, mass),
        )
    log_total = best + jnp.log(mass)
    attended = jnp.zeros((LONG_DEVICE_ROWS, KVH, GROUP, HEAD_SIZE), jnp.float32)
    key_now, value_now = (key3, value3)
    for hop_index in range(SUB):
        if hop_index > 0:
            key_now, value_now = from_behind((key_now, value_now), "ctx", 1)
        attended = lax.cond(
            hop_index <= member,
            lambda acc, kk=key_now, vv=value_now, hh=hop_index: forward_values(
                acc, query4, kk, vv, long_mask(hh), log_total
            ),
            lambda acc: acc,
            attended,
        )
    delta = row_delta(grad4, attended)
    query_gradient = jnp.zeros((LONG_DEVICE_ROWS, KVH, GROUP, HEAD_SIZE), jnp.float32)
    key_gradient = jnp.zeros((LONG_DEVICE_ROWS, KVH, HEAD_SIZE), jnp.float32)
    value_gradient = jnp.zeros((LONG_DEVICE_ROWS, KVH, HEAD_SIZE), jnp.float32)
    key_now, value_now = (key3, value3)
    for hop_index in range(SUB):
        if hop_index > 0:
            key_now, value_now = from_behind((key_now, value_now), "ctx", 1)
            key_gradient, value_gradient = shifted((key_gradient, value_gradient), "ctx", 1)

        def add_parts(totals, kk=key_now, vv=value_now, hh=hop_index):
            part_q, part_k, part_v = backward_block(
                query4, kk, vv, grad4, long_mask(hh), log_total, delta
            )
            return (totals[0] + part_q, totals[1] + part_k, totals[2] + part_v)

        query_gradient, key_gradient, value_gradient = lax.cond(
            hop_index <= member,
            add_parts,
            lambda totals: totals,
            (query_gradient, key_gradient, value_gradient),
        )
    key_gradient, value_gradient = (
        shifted(key_gradient.astype(jnp.bfloat16), "ctx", -(SUB - 1)).astype(key_gradient.dtype),
        shifted(value_gradient.astype(jnp.bfloat16), "ctx", -(SUB - 1)).astype(
            value_gradient.dtype
        ),
    )
    owner_query_gradient = jnp.concatenate(
        [
            query_gradient.reshape(LONG_DEVICE_ROWS, QUERY_HEADS * HEAD_SIZE).astype(jnp.bfloat16),
            short_dq.reshape(SHORT_DEV, QUERY_HEADS * HEAD_SIZE).astype(jnp.bfloat16),
        ],
        axis=0,
    )
    owner_key_gradient = jnp.concatenate(
        [
            key_gradient.reshape(LONG_DEVICE_ROWS, KVH * HEAD_SIZE).astype(jnp.bfloat16),
            short_dk.reshape(SHORT_DEV, KVH * HEAD_SIZE).astype(jnp.bfloat16),
        ],
        axis=0,
    )
    owner_value_gradient = jnp.concatenate(
        [
            value_gradient.reshape(LONG_DEVICE_ROWS, KVH * HEAD_SIZE).astype(jnp.bfloat16),
            short_dv.reshape(SHORT_DEV, KVH * HEAD_SIZE).astype(jnp.bfloat16),
        ],
        axis=0,
    )
    attended_all = jnp.concatenate(
        [
            attended.reshape(LONG_DEVICE_ROWS, QUERY_HEADS * HEAD_SIZE).astype(jnp.bfloat16),
            short_att.reshape(SHORT_DEV, QUERY_HEADS * HEAD_SIZE).astype(jnp.bfloat16),
        ],
        axis=0,
    )
    cot_all = jnp.concatenate([long_c, short_cotangent], axis=0)
    number_of_devices = lax.axis_size("dp") * line_size
    summed_parts = lax.psum_scatter(
        jnp.einsum("ia,ir->ar", attended_all, cot_all, preferred_element_type=jnp.float32),
        ("dp", "ctx"),
        scatter_dimension=0,
        tiled=True,
    )
    adapter_down_gradient = summed_parts * (1.0 / math.sqrt(DEVICE_ROWS * number_of_devices))
    return (owner_query_gradient, owner_key_gradient, owner_value_gradient, adapter_down_gradient)


MESH_ID = pl.DeviceIdType.MESH
F32 = jnp.float32
BF16 = jnp.bfloat16
SLOT_ROWS = 24
PAIR_ROWS = 48
ZS = 4
SCALE = 1.0 / math.sqrt(HEAD_SIZE)
EXP2_SCALE = SCALE / math.log(2.0)


def nn(a, b):
    return lax.dot_general(a, b, (((1,), (0,)), ((), ())), preferred_element_type=F32)


def nt(a, b):
    return lax.dot_general(a, b, (((1,), (1,)), ((), ())), preferred_element_type=F32)


def tn(a, b):
    return lax.dot_general(a, b, (((0,), (0,)), ((), ())), preferred_element_type=F32)


def iota(shape, dim):
    return lax.broadcasted_iota(jnp.int32, shape, dim)


def col_backward(keys_now, values_now, values_t, q_rows, g_rows, bias):
    s = nt(keys_now, q_rows) + bias
    top = jnp.max(s, axis=0, keepdims=True)
    p = jnp.exp2((s - top) * EXP2_SCALE)
    mass = jnp.sum(p, axis=0, keepdims=True)
    w = (p * (1.0 / mass)).astype(BF16)
    att_t = nn(values_t, w)
    dprob = nt(values_now, g_rows)
    w32 = w.astype(F32)
    delta = jnp.sum(w32 * dprob, axis=0, keepdims=True)
    ds = (w32 * (dprob - delta) * SCALE).astype(BF16)
    return w, att_t.astype(BF16), ds


def line_kernel(
    q_ref, k_ref, v_ref, d_ref, og_ref, down_ref, own_ref, slot_ref, len_ref,
    dq_ref, dk_ref, dv_ref, ad_ref,
    kvb, idxb, perm, bias2, pack2, unpack2, w_all, ds_all, q_all, g_all, ogs_bd, bias_s,
    og_t, packed, recv_q, part, recv_a, send_b, recv_b, ad_part, recv_ad, ad_sum, recv_ad2,
    ag_send, ag_recv, ix_send, ix_recv, q_send, q_recv, a_send, a_recv, b_send, b_recv,
    ad_send, ad_recv, ad2_send, ad2_recv,
):
    a = lax.axis_index("dp")
    c = lax.axis_index("ctx")
    z = c // 2
    core = c - 2 * z
    mate = 2 * z + 1 - core

    def sender(src, dst, ssem, rsem, dp, ctx):
        return pltpu.make_async_remote_copy(
            src_ref=src, dst_ref=dst, send_sem=ssem, recv_sem=rsem,
            device_id=(dp, ctx), device_id_type=MESH_ID,
        )

    barrier = pltpu.get_barrier_semaphore()
    for step in range(1, 8):
        pl.semaphore_signal(barrier, inc=1, device_id=(a, lax.rem(c + step, 8)), device_id_type=MESH_ID)
    for step in range(1, 4):
        pl.semaphore_signal(barrier, inc=1, device_id=(lax.rem(a + step, 4), c), device_id_type=MESH_ID)

    for k in range(KVH):
        cols = slice(k * HEAD_SIZE, (k + 1) * HEAD_SIZE)
        kvb[c, k, :, 0:HEAD_SIZE] = k_ref[0:LONG_DEVICE_ROWS, cols]
        kvb[c, k, :, HEAD_SIZE:2 * HEAD_SIZE] = v_ref[0:LONG_DEVICE_ROWS, cols]
    row16 = iota((16, NB), 0)
    own_slot = jnp.where(
        row16 == 0, own_ref[...], jnp.where(row16 == 1, slot_ref[...], 0)
    ).astype(F32).astype(BF16)
    spread = (iota((NB, 128), 0) == lax.shift_right_logical(iota((NB, 128), 1), 1)).astype(F32).astype(BF16)
    idxb[c] = nn(own_slot, spread).astype(BF16)

    pl.semaphore_wait(barrier, 10)

    def kv_copy(way, s, k):
        to = (c + 2, c - 2, mate)[way]
        return sender(kvb.at[s, k], kvb.at[s, k], ag_send.at[way, s, k], ag_recv.at[s, k], a, to)

    def ix_copy(way, s):
        to = (c + 2, c - 2, mate)[way]
        return sender(idxb.at[s], idxb.at[s], ix_send.at[way, s], ix_recv.at[s], a, to)

    def can_send(way, source_z):
        if way == 0:
            return (z < ZS - 1) & (source_z <= z)
        return (z > 0) & (source_z >= z)

    def gather_steps(copy):
        @pl.when(z < ZS - 1)
        def _():
            copy(0, c).start()

        @pl.when(z > 0)
        def _():
            copy(1, c).start()

        copy(2, c).start()

    def gather_hop(copy, hop):
        @pl.when(z >= hop)
        def _():
            s = c - 2 * hop
            copy(2, s).wait_recv()

            @pl.when(z < ZS - 1)
            def _():
                copy(0, s).start()

            copy(2, s).start()

        @pl.when(z + hop < ZS)
        def _():
            s = c + 2 * hop
            copy(2, s).wait_recv()

            @pl.when(z > 0)
            def _():
                copy(1, s).start()

            copy(2, s).start()

    def gather_end(copy):
        for zz in range(ZS):
            copy(2, 2 * zz + 1 - core).wait_recv()

    def gather_drain(copy):
        for hop in range(ZS):
            for sign in ((1,) if hop == 0 else (1, -1)):
                sz = z - sign * hop
                there = (sz >= 0) & (sz < ZS)
                s = c - 2 * sign * hop

                @pl.when(there)
                def _():
                    copy(2, s).wait_send()

                if hop == 0 or sign == 1:
                    @pl.when(there & (z < ZS - 1))
                    def _():
                        copy(0, s).wait_send()

                if hop == 0 or sign == -1:
                    @pl.when(there & (z > 0))
                    def _():
                        copy(1, s).wait_send()

    gather_steps(ix_copy)
    for k in range(KVH):
        gather_steps(lambda way, s, k=k: kv_copy(way, s, k))

    og_long = og_ref[0:LONG_DEVICE_ROWS, :]
    og_short = og_ref[LONG_DEVICE_ROWS:DEVICE_ROWS, :]
    og_t[...] = jnp.transpose(og_long.astype(F32)).astype(BF16)
    rep = ((iota((256, 32), 0) & 31) == iota((256, 32), 1)).astype(F32).astype(BF16)
    ogs_wide = nt(nt(rep, og_short).astype(BF16), rep)
    same = lax.shift_right_logical(iota((256, 256), 0), 5) == lax.shift_right_logical(iota((256, 256), 1), 5)
    ogs_bd[...] = jnp.where(same, ogs_wide, 0.0).astype(BF16)
    e0 = len_ref[0, 0]
    e1 = e0 + len_ref[0, 1]
    e2 = e1 + len_ref[0, 2]

    def segment(ids):
        return sum((ids >= e).astype(jnp.int32) for e in (e0, e1, e2))

    key_id = iota((SHORT_DEV, 256), 0)
    row_id = iota((SHORT_DEV, 256), 1) & 31
    seen = (segment(key_id) == segment(row_id)) & (key_id <= row_id)
    bias_s[...] = jnp.where(seen, 0.0, NEG_FILL)

    for hop in range(1, ZS):
        gather_hop(ix_copy, hop)
    gather_end(ix_copy)
    for k in range(KVH):
        for hop in range(1, ZS):
            gather_hop(lambda way, s, k=k: kv_copy(way, s, k), hop)

    idx = idxb[...].astype(F32)
    lane = iota((1, 128), 1)
    odd = (lane & 1).astype(F32)
    owners = [idx[s, 0:1, :] for s in range(8)]
    places = [owners[s] * 128.0 + idx[s, 1:2, :] * 2.0 + odd for s in range(8)]
    before = (iota((128, 128), 0) < iota((128, 128), 1)).astype(F32).astype(BF16)
    eight = iota((8, 128), 0).astype(F32)
    hot = jnp.concatenate([(eight == owners[s]).astype(F32) for s in range(8)], axis=0)
    counts = hot * nn(hot.astype(BF16), before)
    ranks = [jnp.sum(counts[8 * s:8 * s + 8], axis=0, keepdims=True) for s in range(8)]
    line_id = iota((1024, 128), 0).astype(F32)
    for s in range(8):
        perm[:, s * 128:(s + 1) * 128] = (line_id == places[s]).astype(F32).astype(BF16)

    mine = idxb[c].astype(F32)
    own_mine = mine[0:1, :]
    place_mine = own_mine * 128.0 + mine[1:2, :] * 2.0 + odd
    start_mine = jnp.where(own_mine >= 4.0, 512.0, 0.0)
    bias = jnp.where((line_id >= start_mine) & (line_id <= place_mine), 0.0, NEG_FILL)
    bias2[:, 0:128] = bias
    bias2[:, 128:256] = bias
    hot_mine = (eight == own_mine).astype(F32)
    rank_mine = jnp.sum(hot_mine * nn(hot_mine.astype(BF16), before), axis=0, keepdims=True)
    to_mine = own_mine * SLOT_ROWS + rank_mine
    to_two = jnp.concatenate([to_mine, to_mine], axis=1)
    block = iota((8, PAIR_ROWS, 256), 0)
    within = iota((8, PAIR_ROWS, 256), 1)
    half = (within >= SLOT_ROWS).astype(jnp.int32)
    place = (block * SLOT_ROWS + within - SLOT_ROWS * half).astype(F32)
    lane_half = lax.shift_right_logical(iota((8, PAIR_ROWS, 256), 2), 7)
    hit = (place == to_two[None]) & (half == lane_half)
    pack2[...] = hit.astype(F32).reshape(8 * PAIR_ROWS, 256).astype(BF16)

    me_f = c.astype(F32) * 128.0
    local = iota((128, 128), 0).astype(F32) + me_f
    lands = jnp.concatenate(
        [(local == places[s]).astype(F32).astype(BF16) for s in range(8)], axis=1
    )
    rank_line = jnp.concatenate(ranks, axis=1)
    from_lane = lax.shift_right_logical(iota((8, PAIR_ROWS, 1024), 2), 7) == iota((8, PAIR_ROWS, 1024), 0)
    within_f = iota((8, PAIR_ROWS, 1024), 1).astype(F32)
    for h in range(2):
        holds = (from_lane & (within_f - float(SLOT_ROWS * h) == rank_line[None])).astype(F32)
        holds = holds.reshape(8 * PAIR_ROWS, 1024).astype(BF16)
        unpack2[h * 128:(h + 1) * 128, :] = nt(lands, holds).astype(BF16)

    def head_cols(h):
        return pl.ds(pl.multiple_of(h * HEAD_SIZE, HEAD_SIZE), HEAD_SIZE)

    def grad_head(h, rows, og_rows):
        branch = nt(og_rows, down_ref[pl.ds(pl.multiple_of(h * HEAD_SIZE, HEAD_SIZE), HEAD_SIZE), :])
        return (d_ref[rows, head_cols(h)].astype(F32) + branch).astype(BF16)

    long_rows = slice(0, LONG_DEVICE_ROWS)
    short_rows = slice(LONG_DEVICE_ROWS, DEVICE_ROWS)

    def a_copy(k):
        return sender(part.at[k, 1 - core], recv_a.at[k], a_send.at[k], a_recv.at[k], a, mate)

    def b_copy(k, step):
        to = lax.rem(z + step, ZS)
        return sender(send_b.at[k, to], recv_b.at[k, z], b_send.at[k, to], b_recv.at[k, z], a, 2 * to + core)

    def b_landed(k, step):
        frm = lax.rem(z + step, ZS)
        return sender(send_b.at[k, frm], recv_b.at[k, frm], b_send.at[k, frm], b_recv.at[k, frm], a, 2 * frm + core)

    def q_copy(k, step):
        to = lax.rem(c + step, 8)
        return sender(packed.at[k, to], recv_q.at[k, c], q_send.at[k, to], q_recv.at[k, c], a, to)

    def q_landed(k, step):
        frm = lax.rem(c + step, 8)
        return sender(packed.at[k, frm], recv_q.at[k, frm], q_send.at[k, frm], q_recv.at[k, frm], a, frm)

    def ad_copy(k):
        return sender(ad_part.at[k], recv_ad.at[a], ad_send.at[k], ad_recv.at[a], k, c)

    def ad_landed(step):
        frm = lax.rem(a + step, 4)
        return sender(ad_part.at[frm], recv_ad.at[frm], ad_send.at[frm], ad_recv.at[frm], frm, c)

    def ad2_copy(step):
        to = lax.rem(c + step, 8)
        return sender(ad_sum.at[to], recv_ad2.at[c], ad2_send.at[to], ad2_recv.at[c], a, to)

    def ad2_landed(step):
        frm = lax.rem(c + step, 8)
        return sender(ad_sum.at[frm], recv_ad2.at[frm], ad2_send.at[frm], ad2_recv.at[frm], a, frm)

    def chip_sum(k):
        a_copy(k).wait_recv()
        total = part[k, core].astype(F32) + recv_a[k].astype(F32)
        send_b[k] = total.astype(BF16)
        for step in range(1, ZS):
            b_copy(k, step).start()

    def group(k, carry):
        for zz in range(ZS):
            kv_copy(2, 2 * zz + 1 - core, k).wait_recv()
        blocks = jnp.concatenate([kvb[s, k] for s in range(8)], axis=0)
        ordered = nn(perm[...], blocks)
        ordered_t = jnp.transpose(ordered)
        key_o = ordered[:, 0:128].astype(BF16)
        val_o = ordered[:, 128:256].astype(BF16)
        key_t = ordered_t[0:128].astype(BF16)
        val_t = ordered_t[128:256].astype(BF16)

        ks = k_ref[short_rows, head_cols(k)]
        vs = v_ref[short_rows, head_cols(k)]
        qs = jnp.concatenate([q_ref[short_rows, head_cols(k * GROUP + g)] for g in range(GROUP)], axis=0)
        gs = jnp.concatenate([grad_head(k * GROUP + g, short_rows, og_short) for g in range(GROUP)], axis=0)
        vs_t = jnp.transpose(vs.astype(F32)).astype(BF16)
        w, att_t, ds = col_backward(ks, vs, vs_t, qs, gs, bias_s[...])
        dqs = tn(ds, ks).astype(BF16)
        for g in range(GROUP):
            dq_ref[short_rows, head_cols(k * GROUP + g)] = dqs[g * SHORT_DEV:(g + 1) * SHORT_DEV]
        dk_ref[short_rows, head_cols(k)] = nn(ds, qs).astype(BF16)
        dv_ref[short_rows, head_cols(k)] = nn(w, gs).astype(BF16)
        ad_part[k] = nt(ogs_bd[...], att_t).reshape(GROUP, ADAPTER_RANK, HEAD_SIZE)

        for p in range(4):
            heads = (k * GROUP + 2 * p, k * GROUP + 2 * p + 1)
            qp = jnp.concatenate([q_ref[long_rows, head_cols(h)] for h in heads], axis=0)
            gp = jnp.concatenate([grad_head(h, long_rows, og_long) for h in heads], axis=0)
            w, att_t, ds = col_backward(key_o, val_o, val_t, qp, gp, bias2[...])
            cols = slice(p * 256, (p + 1) * 256)
            w_all[:, cols] = w
            ds_all[:, cols] = ds
            q_all[cols, :] = qp
            g_all[cols, :] = gp
            dq_t = nn(key_t, ds).astype(BF16)
            packed[k, :, :, p * 128:(p + 1) * 128] = (
                nt(pack2[...], dq_t).astype(BF16).reshape(8, PAIR_ROWS, HEAD_SIZE)
            )
            for h in range(2):
                ad_part[k, 2 * p + h] += nt(og_t[...], att_t[:, h * 128:(h + 1) * 128])

        for step in range(1, 8):
            q_copy(k, step).start()
        recv_q[k, c] = packed[k, c]

        dk = nn(ds_all[...], q_all[...]).astype(BF16).reshape(ZS, 2, 128, HEAD_SIZE)
        dv = nn(w_all[...], g_all[...]).astype(BF16).reshape(ZS, 2, 128, HEAD_SIZE)
        for zz in range(ZS):
            for cc in range(2):
                part[k, cc, zz, :, 0:128] = dk[zz, cc]
                part[k, cc, zz, :, 128:256] = dv[zz, cc]
        a_copy(k).start()

        @pl.when(k != a)
        def _():
            ad_copy(k).start()

        @pl.when(k > 0)
        def _():
            chip_sum(k - 1)

        return carry

    lax.fori_loop(0, KVH, group, 0)
    chip_sum(KVH - 1)

    for step in range(1, 4):
        ad_landed(step).wait_recv()
    recv_ad[a] = ad_part[a]
    total = recv_ad[0] + recv_ad[1] + recv_ad[2] + recv_ad[3]
    ad_sum[...] = total.astype(BF16)
    for step in range(1, 8):
        ad2_copy(step).start()
    recv_ad2[c] = ad_sum[c]

    def finish(k, carry):
        for step in range(1, 8):
            q_landed(k, step).wait_recv()
        rows = nn(unpack2[...], recv_q[k].reshape(8 * PAIR_ROWS, 512)).astype(BF16)
        for p in range(4):
            for h in range(2):
                dq_ref[long_rows, head_cols(k * GROUP + 2 * p + h)] = rows[
                    h * 128:(h + 1) * 128, p * 128:(p + 1) * 128
                ]
        total = send_b[k, z].astype(F32)
        for step in range(1, ZS):
            b_landed(k, step).wait_recv()
            total += recv_b[k, lax.rem(z + step, ZS)].astype(F32)
        dk_ref[long_rows, head_cols(k)] = total[:, 0:128].astype(BF16)
        dv_ref[long_rows, head_cols(k)] = total[:, 128:256].astype(BF16)
        return carry

    lax.fori_loop(0, KVH, finish, 0)

    for step in range(1, 8):
        ad2_landed(step).wait_recv()
    total = recv_ad2[0].astype(F32)
    for s in range(1, 8):
        total += recv_ad2[s].astype(F32)
    ad_ref[...] = jnp.transpose(total) * (1.0 / math.sqrt(DEVICE_ROWS * 32))

    gather_drain(ix_copy)

    def drain(k, carry):
        gather_drain(lambda way, s: kv_copy(way, s, k))
        for step in range(1, 8):
            q_copy(k, step).wait_send()
        a_copy(k).wait_send()
        for step in range(1, ZS):
            b_copy(k, step).wait_send()

        @pl.when(k != a)
        def _():
            ad_copy(k).wait_send()

        return carry

    lax.fori_loop(0, KVH, drain, 0)
    for step in range(1, 8):
        ad2_copy(step).wait_send()


def line_shards(q, k, v, d, og, down, own, slot, lengths):
    vmem = pl.BlockSpec(memory_space=pltpu.VMEM)
    smem = pl.BlockSpec(memory_space=pltpu.SMEM)
    dma = pltpu.SemaphoreType.DMA
    return pl.pallas_call(
        line_kernel,
        out_shape=(
            jax.ShapeDtypeStruct((DEVICE_ROWS, QUERY_HEADS * HEAD_SIZE), BF16),
            jax.ShapeDtypeStruct((DEVICE_ROWS, KVH * HEAD_SIZE), BF16),
            jax.ShapeDtypeStruct((DEVICE_ROWS, KVH * HEAD_SIZE), BF16),
            jax.ShapeDtypeStruct((HEAD_SIZE, ADAPTER_RANK), F32),
        ),
        in_specs=[vmem] * 8 + [smem],
        out_specs=[vmem] * 4,
        scratch_shapes=[
            pltpu.VMEM((8, KVH, 128, 256), BF16),
            pltpu.VMEM((8, 16, 128), BF16),
            pltpu.VMEM((1024, 1024), BF16),
            pltpu.VMEM((1024, 256), F32),
            pltpu.VMEM((8 * PAIR_ROWS, 256), BF16),
            pltpu.VMEM((256, 8 * PAIR_ROWS), BF16),
            pltpu.VMEM((1024, 1024), BF16),
            pltpu.VMEM((1024, 1024), BF16),
            pltpu.VMEM((1024, 128), BF16),
            pltpu.VMEM((1024, 128), BF16),
            pltpu.VMEM((256, 256), BF16),
            pltpu.VMEM((SHORT_DEV, 256), F32),
            pltpu.VMEM((ADAPTER_RANK, 128), BF16),
            pltpu.VMEM((KVH, 8, PAIR_ROWS, 512), BF16),
            pltpu.VMEM((KVH, 8, PAIR_ROWS, 512), BF16),
            pltpu.VMEM((KVH, 2, ZS, 128, 256), BF16),
            pltpu.VMEM((KVH, ZS, 128, 256), BF16),
            pltpu.VMEM((KVH, ZS, 128, 256), BF16),
            pltpu.VMEM((KVH, ZS, 128, 256), BF16),
            pltpu.VMEM((KVH, GROUP, ADAPTER_RANK, HEAD_SIZE), F32),
            pltpu.VMEM((4, GROUP, ADAPTER_RANK, HEAD_SIZE), F32),
            pltpu.VMEM((8, ADAPTER_RANK, HEAD_SIZE), BF16),
            pltpu.VMEM((8, ADAPTER_RANK, HEAD_SIZE), BF16),
            dma((3, 8, KVH)), dma((8, KVH)),
            dma((3, 8)), dma((8,)),
            dma((KVH, 8)), dma((KVH, 8)),
            dma((KVH,)), dma((KVH,)),
            dma((KVH, ZS)), dma((KVH, ZS)),
            dma((4,)), dma((4,)),
            dma((8,)), dma((8,)),
        ],
        compiler_params=pltpu.CompilerParams(
            collective_id=0, has_side_effects=True, vmem_limit_bytes=56 * 1024 * 1024
        ),
        cost_estimate=pl.CostEstimate(flops=10 ** 10, bytes_accessed=8 * 10 ** 6, transcendentals=4 * 10 ** 6),
    )(q, k, v, d, og, down, own, slot, lengths)


def solution(mesh):
    in_specs = (
        P(("dp", "ctx"), None),
        P(("dp", "ctx"), None),
        P(("dp", "ctx"), None),
        P(("dp", "ctx"), None),
        P(("dp", "ctx"), None),
        P(),
        P(("dp", "ctx"), None),
        P(("dp", "ctx"), None),
        P(("dp", "ctx"), None),
    )
    out_specs = (
        P(("dp", "ctx"), None),
        P(("dp", "ctx"), None),
        P(("dp", "ctx"), None),
        P(("dp", "ctx"), None),
    )
    body = line_shards if dict(mesh.shape) == {"dp": 4, "ctx": 8} else shards
    return jax.shard_map(body, mesh=mesh, in_specs=in_specs, out_specs=out_specs, check_vma=False)
```

profile of v0, /device:TPU:0, one launch (start us, length us, event | category | flops | bytes accessed | tf_op | source)
XLA Modules:
  0.0 109.1 jit_solution(436073409862787112)
XLA Ops:
  0.6 1.4 %copy.13.og_ref = bf16[160,32]{1,0:T(8,128)(2,1)} copy(bf16[160,32]{0,1:T(8,128)(2,1)} %param.13) | data formatting | bytes 20480 | tf_op args[4]
  2.1 2.3 %copy.14.down_ref = bf16[4096,32]{1,0:T(8,128)(2,1)} copy(bf16[4096,32]{0,1:T(8,128)(2,1)} %param.14) | data formatting | bytes 524288 | tf_op args[5]
  4.3 99.4 %shard_map.120 = (bf16[160,4096]{1,0:T(8,128)(2,1)}, bf16[160,512]{1,0:T(8,128)(2,1)}, bf16[160,512]{1,0:T(8,128)(2,1)}, f32[128,32]{1,0:T(8,128)}) custom-call(bf16[160,4096]{1,0:T(8,128)(2,1)} %q_ref.1, bf16[160,512]{1,0:T(8,128)(2,1)} %k_ref.1, bf16[160,512]{1,0:T(8,128)(2,1)} %v_ref.1, bf16[160,4096]{1,0:T(8,128)(2,1)} %d_ref.1, ...), custom_call_target="tpu_custom_call" | custom-call | flops 10000000000 | bytes 8000000 | tf_op jit(solution)/shard_map/pallas_call | solution.py:690
  103.7 1.5 %copy.15 = f32[128,32]{0,1:T(8,128)} copy(f32[128,32]{1,0:T(8,128)} %get-tuple-element.7) | data formatting | bytes 32768 | tf_op jit(solution)/shard_map/pallas_call | solution.py:690
  105.2 0.0 copy-start.1
  105.2 0.0 copy-start
  105.2 2.5 %copy.19 = bf16[160,4096]{1,0:T(8,128)(2,1)} copy(bf16[160,4096]{1,0:T(8,128)(2,1)} %get-tuple-element.12) | data formatting | bytes 2621440
  107.8 0.0 copy-done.1
  107.8 0.7 copy.20
  108.4 0.0 copy-done
  108.4 0.7 copy.21
Async XLA Ops:
  105.2 2.5 %copy-start.1 = (bf16[160,512]{1,0:T(8,128)(2,1)S(1)}, bf16[160,512]{1,0:T(8,128)(2,1)}, u32[]{:S(2)}) copy-start(bf16[160,512]{1,0:T(8,128)(2,1)} %get-tuple-element.13) | copy-start | bytes 491524
  105.2 3.2 %copy-start = (bf16[160,512]{1,0:T(8,128)(2,1)S(1)}, bf16[160,512]{1,0:T(8,128)(2,1)}, u32[]{:S(2)}) copy-start(bf16[160,512]{1,0:T(8,128)(2,1)} %get-tuple-element.14) | copy-start | bytes 491524
where the time goes:
time: 109 us
  Pallas kernels  99.4 us (91%)
  local copies, waits for them, and re-layouts  9.1 us (8%)
    pallas_call x1, Pallas kernels, line_shards(): pl.pallas_call(line_kernel, out_shape=(jax.ShapeDtypeStruct((DEVICE_ROWS,...  99.4 us
    unnamed x9, local copies, waits for them, and re-layouts  7.58 us

commit v1 on v0

--- a/solution.py
+++ b/solution.py
@@ -309,13 +309,13 @@
     return lax.broadcasted_iota(jnp.int32, shape, dim)
 
 
-def col_backward(keys_now, values_now, values_t, q_rows, g_rows, bias):
+def col_backward(keys_now, values_now, values_t, q_rows, g_rows, bias, pick):
     s = nt(keys_now, q_rows) + bias
     top = jnp.max(s, axis=0, keepdims=True)
     p = jnp.exp2((s - top) * EXP2_SCALE)
     mass = jnp.sum(p, axis=0, keepdims=True)
     w = (p * (1.0 / mass)).astype(BF16)
-    att_t = nn(values_t, w)
+    att_t = pick(nn(values_t, w))
     dprob = nt(values_now, g_rows)
     w32 = w.astype(F32)
     delta = jnp.sum(w32 * dprob, axis=0, keepdims=True)
@@ -326,8 +326,8 @@
 def line_kernel(
     q_ref, k_ref, v_ref, d_ref, og_ref, down_ref, own_ref, slot_ref, len_ref,
     dq_ref, dk_ref, dv_ref, ad_ref,
-    kvb, idxb, perm, bias2, pack2, unpack2, w_all, ds_all, q_all, g_all, ogs_bd, bias_s,
-    og_t, packed, recv_q, part, recv_a, send_b, recv_b, ad_part, recv_ad, ad_sum, recv_ad2,
+    kvb, idxb, perm, bias2, in_second, row_half, pack2, unpack2, w_all, ds_all, q_all, g_all, ogs_bd, bias_s,
+    og_t, packed, recv_q, part, recv_a, send_b, recv_b, b_total, ad_part, recv_ad, ad_sum, recv_ad2,
     ag_send, ag_recv, ix_send, ix_recv, q_send, q_recv, a_send, a_recv, b_send, b_recv,
     ad_send, ad_recv, ad2_send, ad2_recv,
 ):
@@ -434,13 +434,16 @@
                     def _():
                         copy(1, s).wait_send()
 
+    def kv_chunk(k):
+        return lambda way, s: kv_copy(way, s, k)
+
     gather_steps(ix_copy)
-    for k in range(KVH):
-        gather_steps(lambda way, s, k=k: kv_copy(way, s, k))
-
-    og_long = og_ref[0:LONG_DEVICE_ROWS, :]
-    og_short = og_ref[LONG_DEVICE_ROWS:DEVICE_ROWS, :]
-    og_t[...] = jnp.transpose(og_long.astype(F32)).astype(BF16)
+    gather_steps(kv_chunk(0))
+
+    og_rows_all = jnp.transpose(og_ref[...].astype(F32)).astype(BF16)
+    og_long = og_rows_all[0:LONG_DEVICE_ROWS]
+    og_short = og_rows_all[LONG_DEVICE_ROWS:DEVICE_ROWS]
+    og_t[...] = og_ref[:, 0:LONG_DEVICE_ROWS]
     rep = ((iota((256, 32), 0) & 31) == iota((256, 32), 1)).astype(F32).astype(BF16)
     ogs_wide = nt(nt(rep, og_short).astype(BF16), rep)
     same = lax.shift_right_logical(iota((256, 256), 0), 5) == lax.shift_right_logical(iota((256, 256), 1), 5)
@@ -457,12 +460,37 @@
     seen = (segment(key_id) == segment(row_id)) & (key_id <= row_id)
     bias_s[...] = jnp.where(seen, 0.0, NEG_FILL)
 
+    def head_cols(h):
+        return pl.ds(pl.multiple_of(h * HEAD_SIZE, HEAD_SIZE), HEAD_SIZE)
+
+    def grad_head(h, rows, og_rows):
+        branch = nn(og_rows, down_ref[:, head_cols(h)])
+        return (d_ref[rows, head_cols(h)].astype(F32) + branch).astype(BF16)
+
+    long_rows = slice(0, LONG_DEVICE_ROWS)
+    short_rows = slice(LONG_DEVICE_ROWS, DEVICE_ROWS)
+
+    def short_group(k):
+        ks = k_ref[short_rows, head_cols(k)]
+        vs = v_ref[short_rows, head_cols(k)]
+        qs = jnp.concatenate([q_ref[short_rows, head_cols(k * GROUP + g)] for g in range(GROUP)], axis=0)
+        gs = jnp.concatenate([grad_head(k * GROUP + g, short_rows, og_short) for g in range(GROUP)], axis=0)
+        vs_t = jnp.transpose(vs.astype(F32)).astype(BF16)
+        w, att_t, ds = col_backward(ks, vs, vs_t, qs, gs, bias_s[...], lambda x: x)
+        dqs = tn(ds, ks).astype(BF16)
+        for g in range(GROUP):
+            dq_ref[short_rows, head_cols(k * GROUP + g)] = dqs[g * SHORT_DEV:(g + 1) * SHORT_DEV]
+        dk_ref[short_rows, head_cols(k)] = nn(ds, qs).astype(BF16)
+        dv_ref[short_rows, head_cols(k)] = nn(w, gs).astype(BF16)
+        ad_part[k] = nt(ogs_bd[...], att_t).reshape(GROUP, ADAPTER_RANK, HEAD_SIZE)
+
+    short_group(0)
     for hop in range(1, ZS):
         gather_hop(ix_copy, hop)
+        gather_hop(kv_chunk(0), hop)
+        short_group(hop)
+    gather_steps(kv_chunk(1))
     gather_end(ix_copy)
-    for k in range(KVH):
-        for hop in range(1, ZS):
-            gather_hop(lambda way, s, k=k: kv_copy(way, s, k), hop)
 
     idx = idxb[...].astype(F32)
     lane = iota((1, 128), 1)
@@ -482,9 +510,16 @@
     own_mine = mine[0:1, :]
     place_mine = own_mine * 128.0 + mine[1:2, :] * 2.0 + odd
     start_mine = jnp.where(own_mine >= 4.0, 512.0, 0.0)
-    bias = jnp.where((line_id >= start_mine) & (line_id <= place_mine), 0.0, NEG_FILL)
+    at_mine = place_mine - start_mine
+    bias = jnp.where(line_id[0:512] <= at_mine, 0.0, NEG_FILL)
     bias2[:, 0:128] = bias
     bias2[:, 128:256] = bias
+    second = (own_mine >= 4.0).astype(F32)
+    second_two = jnp.concatenate([second, second], axis=1)
+    in_second[...] = jnp.broadcast_to(second_two, (128, 256))
+    second_rows = jnp.transpose(jnp.broadcast_to(second, (128, 128)))
+    row_half[:, 0:128] = (1.0 - second_rows).astype(BF16)
+    row_half[:, 128:256] = second_rows.astype(BF16)
     hot_mine = (eight == own_mine).astype(F32)
     rank_mine = jnp.sum(hot_mine * nn(hot_mine.astype(BF16), before), axis=0, keepdims=True)
     to_mine = own_mine * SLOT_ROWS + rank_mine
@@ -497,6 +532,151 @@
     hit = (place == to_two[None]) & (half == lane_half)
     pack2[...] = hit.astype(F32).reshape(8 * PAIR_ROWS, 256).astype(BF16)
 
+    def a_copy(k):
+        return sender(part.at[k, 1 - core], recv_a.at[k], a_send.at[k], a_recv.at[k], a, mate)
+
+    def b_copy(way, k, zz):
+        to = c + 2 if way == 0 else c - 2
+        return sender(
+            send_b.at[way, k, zz], recv_b.at[way, k, zz], b_send.at[way, k, zz], b_recv.at[way, k, zz], a, to
+        )
+
+    def b_landed(way, k, zz):
+        return sender(
+            send_b.at[way, k, zz], recv_b.at[way, k, zz], b_send.at[way, k, zz], b_recv.at[way, k, zz], a, mate
+        )
+
+    def q_copy(k, step):
+        to = lax.rem(c + step, 8)
+        return sender(packed.at[k, to], recv_q.at[k, c], q_send.at[k, to], q_recv.at[k, c], a, to)
+
+    def q_landed(k, step):
+        frm = lax.rem(c + step, 8)
+        return sender(packed.at[k, frm], recv_q.at[k, frm], q_send.at[k, frm], q_recv.at[k, frm], a, frm)
+
+    def ad_copy(k):
+        return sender(ad_part.at[k], recv_ad.at[a], ad_send.at[k], ad_recv.at[a], k, c)
+
+    def ad_landed(step):
+        frm = lax.rem(a + step, 4)
+        return sender(ad_part.at[frm], recv_ad.at[frm], ad_send.at[frm], ad_recv.at[frm], frm, c)
+
+    def ad2_copy(step):
+        to = lax.rem(c + step, 8)
+        return sender(ad_sum.at[to], recv_ad2.at[c], ad2_send.at[to], ad2_recv.at[c], a, to)
+
+    def ad2_landed(step):
+        frm = lax.rem(c + step, 8)
+        return sender(ad_sum.at[frm], recv_ad2.at[frm], ad2_send.at[frm], ad2_recv.at[frm], a, frm)
+
+    def chip_sum(k):
+        a_copy(k).wait_recv()
+        part[k, core] = (part[k, core].astype(F32) + recv_a[k].astype(F32)).astype(BF16)
+
+        @pl.when(z == 0)
+        def _():
+            for zz in range(1, ZS):
+                send_b[0, k, zz] = part[k, core, zz]
+                b_copy(0, k, zz).start()
+
+        @pl.when(z == ZS - 1)
+        def _():
+            for zz in range(ZS - 1):
+                send_b[1, k, zz] = part[k, core, zz]
+                b_copy(1, k, zz).start()
+
+    def line_sum(k, hop):
+        def pass_on(way, zz):
+            b_landed(way, k, zz).wait_recv()
+            send_b[way, k, zz] = (part[k, core, zz].astype(F32) + recv_b[way, k, zz].astype(F32)).astype(BF16)
+            b_copy(way, k, zz).start()
+
+        @pl.when(z == hop)
+        def _():
+            for zz in range(hop + 1, ZS):
+                pass_on(0, zz)
+
+        @pl.when(z == ZS - 1 - hop)
+        def _():
+            for zz in range(ZS - 1 - hop):
+                pass_on(1, zz)
+
+    def group(k, carry):
+        for zz in range(ZS):
+            kv_copy(2, 2 * zz + 1 - core, k).wait_recv()
+        blocks = jnp.concatenate([kvb[s, k] for s in range(8)], axis=0)
+        ordered = nn(perm[...], blocks)
+        key_w = jnp.concatenate([ordered[0:512, 0:128], ordered[512:1024, 0:128]], axis=1)
+        val_w = jnp.concatenate([ordered[0:512, 128:256], ordered[512:1024, 128:256]], axis=1)
+        key_t = jnp.transpose(key_w).astype(BF16)
+        val_t = jnp.transpose(val_w).astype(BF16)
+        key_o = key_w.astype(BF16)
+        val_o = val_w.astype(BF16)
+        halves = row_half[...]
+        halves = jnp.concatenate([halves, halves], axis=0)
+
+        def pick(x):
+            return jnp.where(in_second[...] > 0.5, x[128:256], x[0:128])
+
+        def widen(x):
+            return jnp.concatenate([x, x], axis=1) * halves
+
+        for p in range(4):
+            heads = (k * GROUP + 2 * p, k * GROUP + 2 * p + 1)
+            qp = jnp.concatenate([q_ref[long_rows, head_cols(h)] for h in heads], axis=0)
+            gp = jnp.concatenate([grad_head(h, long_rows, og_long) for h in heads], axis=0)
+            qp, gp = widen(qp), widen(gp)
+            w, att_t, ds = col_backward(key_o, val_o, val_t, qp, gp, bias2[...], pick)
+            cols = slice(p * 256, (p + 1) * 256)
+            w_all[:, cols] = w
+            ds_all[:, cols] = ds
+            q_all[cols, :] = qp
+            g_all[cols, :] = gp
+            dq_t = pick(nn(key_t, ds)).astype(BF16)
+            packed[k, :, :, p * 128:(p + 1) * 128] = (
+                nt(pack2[...], dq_t).astype(BF16).reshape(8, PAIR_ROWS, HEAD_SIZE)
+            )
+            for h in range(2):
+                ad_part[k, 2 * p + h] += nt(og_t[...], att_t[:, h * 128:(h + 1) * 128])
+
+            @pl.when(k < KVH - 1)
+            def _(p=p):
+                if p == 0:
+                    @pl.when(k < KVH - 2)
+                    def _():
+                        gather_steps(kv_chunk(k + 2))
+                else:
+                    gather_hop(kv_chunk(k + 1), p)
+
+            @pl.when(k > 0)
+            def _(p=p):
+                if p == 0:
+                    chip_sum(k - 1)
+                else:
+                    line_sum(k - 1, p)
+
+        dk = nn(ds_all[...], q_all[...]).astype(BF16)
+        dv = nn(w_all[...], g_all[...]).astype(BF16)
+        for zz in range(ZS):
+            for cc in range(2):
+                owner = 2 * zz + cc
+                rows = slice((owner % 4) * 128, (owner % 4) * 128 + 128)
+                cols = slice((owner // 4) * 128, (owner // 4) * 128 + 128)
+                part[k, cc, zz, :, 0:128] = dk[rows, cols]
+                part[k, cc, zz, :, 128:256] = dv[rows, cols]
+        a_copy(k).start()
+        for step in range(1, 8):
+            q_copy(k, step).start()
+        recv_q[k, c] = packed[k, c]
+
+        @pl.when(k != a)
+        def _():
+            ad_copy(k).start()
+
+        return carry
+
+    lax.fori_loop(0, KVH, group, 0)
+
     me_f = c.astype(F32) * 128.0
     local = iota((128, 128), 0).astype(F32) + me_f
     lands = jnp.concatenate(
@@ -510,121 +690,6 @@
         holds = holds.reshape(8 * PAIR_ROWS, 1024).astype(BF16)
         unpack2[h * 128:(h + 1) * 128, :] = nt(lands, holds).astype(BF16)
 
-    def head_cols(h):
-        return pl.ds(pl.multiple_of(h * HEAD_SIZE, HEAD_SIZE), HEAD_SIZE)
-
-    def grad_head(h, rows, og_rows):
-        branch = nt(og_rows, down_ref[pl.ds(pl.multiple_of(h * HEAD_SIZE, HEAD_SIZE), HEAD_SIZE), :])
-        return (d_ref[rows, head_cols(h)].astype(F32) + branch).astype(BF16)
-
-    long_rows = slice(0, LONG_DEVICE_ROWS)
-    short_rows = slice(LONG_DEVICE_ROWS, DEVICE_ROWS)
-
-    def a_copy(k):
-        return sender(part.at[k, 1 - core], recv_a.at[k], a_send.at[k], a_recv.at[k], a, mate)
-
-    def b_copy(k, step):
-        to = lax.rem(z + step, ZS)
-        return sender(send_b.at[k, to], recv_b.at[k, z], b_send.at[k, to], b_recv.at[k, z], a, 2 * to + core)
-
-    def b_landed(k, step):
-        frm = lax.rem(z + step, ZS)
-        return sender(send_b.at[k, frm], recv_b.at[k, frm], b_send.at[k, frm], b_recv.at[k, frm], a, 2 * frm + core)
-
-    def q_copy(k, step):
-        to = lax.rem(c + step, 8)
-        return sender(packed.at[k, to], recv_q.at[k, c], q_send.at[k, to], q_recv.at[k, c], a, to)
-
-    def q_landed(k, step):
-        frm = lax.rem(c + step, 8)
-        return sender(packed.at[k, frm], recv_q.at[k, frm], q_send.at[k, frm], q_recv.at[k, frm], a, frm)
-
-    def ad_copy(k):
-        return sender(ad_part.at[k], recv_ad.at[a], ad_send.at[k], ad_recv.at[a], k, c)
-
-    def ad_landed(step):
-        frm = lax.rem(a + step, 4)
-        return sender(ad_part.at[frm], recv_ad.at[frm], ad_send.at[frm], ad_recv.at[frm], frm, c)
-
-    def ad2_copy(step):
-        to = lax.rem(c + step, 8)
-        return sender(ad_sum.at[to], recv_ad2.at[c], ad2_send.at[to], ad2_recv.at[c], a, to)
-
-    def ad2_landed(step):
-        frm = lax.rem(c + step, 8)
-        return sender(ad_sum.at[frm], recv_ad2.at[frm], ad2_send.at[frm], ad2_recv.at[frm], a, frm)
-
-    def chip_sum(k):
-        a_copy(k).wait_recv()
-        total = part[k, core].astype(F32) + recv_a[k].astype(F32)
-        send_b[k] = total.astype(BF16)
-        for step in range(1, ZS):
-            b_copy(k, step).start()
-
-    def group(k, carry):
-        for zz in range(ZS):
-            kv_copy(2, 2 * zz + 1 - core, k).wait_recv()
-        blocks = jnp.concatenate([kvb[s, k] for s in range(8)], axis=0)
-        ordered = nn(perm[...], blocks)
-        ordered_t = jnp.transpose(ordered)
-        key_o = ordered[:, 0:128].astype(BF16)
-        val_o = ordered[:, 128:256].astype(BF16)
-        key_t = ordered_t[0:128].astype(BF16)
-        val_t = ordered_t[128:256].astype(BF16)
-
-        ks = k_ref[short_rows, head_cols(k)]
-        vs = v_ref[short_rows, head_cols(k)]
-        qs = jnp.concatenate([q_ref[short_rows, head_cols(k * GROUP + g)] for g in range(GROUP)], axis=0)
-        gs = jnp.concatenate([grad_head(k * GROUP + g, short_rows, og_short) for g in range(GROUP)], axis=0)
-        vs_t = jnp.transpose(vs.astype(F32)).astype(BF16)
-        w, att_t, ds = col_backward(ks, vs, vs_t, qs, gs, bias_s[...])
-        dqs = tn(ds, ks).astype(BF16)
-        for g in range(GROUP):
-            dq_ref[short_rows, head_cols(k * GROUP + g)] = dqs[g * SHORT_DEV:(g + 1) * SHORT_DEV]
-        dk_ref[short_rows, head_cols(k)] = nn(ds, qs).astype(BF16)
-        dv_ref[short_rows, head_cols(k)] = nn(w, gs).astype(BF16)
-        ad_part[k] = nt(ogs_bd[...], att_t).reshape(GROUP, ADAPTER_RANK, HEAD_SIZE)
-
-        for p in range(4):
-            heads = (k * GROUP + 2 * p, k * GROUP + 2 * p + 1)
-            qp = jnp.concatenate([q_ref[long_rows, head_cols(h)] for h in heads], axis=0)
-            gp = jnp.concatenate([grad_head(h, long_rows, og_long) for h in heads], axis=0)
-            w, att_t, ds = col_backward(key_o, val_o, val_t, qp, gp, bias2[...])
-            cols = slice(p * 256, (p + 1) * 256)
-            w_all[:, cols] = w
-            ds_all[:, cols] = ds
-            q_all[cols, :] = qp
-            g_all[cols, :] = gp
-            dq_t = nn(key_t, ds).astype(BF16)
-            packed[k, :, :, p * 128:(p + 1) * 128] = (
-                nt(pack2[...], dq_t).astype(BF16).reshape(8, PAIR_ROWS, HEAD_SIZE)
-            )
-            for h in range(2):
-                ad_part[k, 2 * p + h] += nt(og_t[...], att_t[:, h * 128:(h + 1) * 128])
-
-        for step in range(1, 8):
-            q_copy(k, step).start()
-        recv_q[k, c] = packed[k, c]
-
-        dk = nn(ds_all[...], q_all[...]).astype(BF16).reshape(ZS, 2, 128, HEAD_SIZE)
-        dv = nn(w_all[...], g_all[...]).astype(BF16).reshape(ZS, 2, 128, HEAD_SIZE)
-        for zz in range(ZS):
-            for cc in range(2):
-                part[k, cc, zz, :, 0:128] = dk[zz, cc]
-                part[k, cc, zz, :, 128:256] = dv[zz, cc]
-        a_copy(k).start()
-
-        @pl.when(k != a)
-        def _():
-            ad_copy(k).start()
-
-        @pl.when(k > 0)
-        def _():
-            chip_sum(k - 1)
-
-        return carry
-
-    lax.fori_loop(0, KVH, group, 0)
     chip_sum(KVH - 1)
 
     for step in range(1, 4):
@@ -635,6 +700,9 @@
     for step in range(1, 8):
         ad2_copy(step).start()
     recv_ad2[c] = ad_sum[c]
+
+    for hop in range(1, ZS):
+        line_sum(KVH - 1, hop)
 
     def finish(k, carry):
         for step in range(1, 8):
@@ -645,12 +713,20 @@
                 dq_ref[long_rows, head_cols(k * GROUP + 2 * p + h)] = rows[
                     h * 128:(h + 1) * 128, p * 128:(p + 1) * 128
                 ]
-        total = send_b[k, z].astype(F32)
-        for step in range(1, ZS):
-            b_landed(k, step).wait_recv()
-            total += recv_b[k, lax.rem(z + step, ZS)].astype(F32)
-        dk_ref[long_rows, head_cols(k)] = total[:, 0:128].astype(BF16)
-        dv_ref[long_rows, head_cols(k)] = total[:, 128:256].astype(BF16)
+        b_total[...] = part[k, core, z].astype(F32)
+
+        @pl.when(z > 0)
+        def _():
+            b_landed(0, k, z).wait_recv()
+            b_total[...] += recv_b[0, k, z].astype(F32)
+
+        @pl.when(z < ZS - 1)
+        def _():
+            b_landed(1, k, z).wait_recv()
+            b_total[...] += recv_b[1, k, z].astype(F32)
+
+        dk_ref[long_rows, head_cols(k)] = b_total[:, 0:128].astype(BF16)
+        dv_ref[long_rows, head_cols(k)] = b_total[:, 128:256].astype(BF16)
         return carry
 
     lax.fori_loop(0, KVH, finish, 0)
@@ -660,7 +736,7 @@
     total = recv_ad2[0].astype(F32)
     for s in range(1, 8):
         total += recv_ad2[s].astype(F32)
-    ad_ref[...] = jnp.transpose(total) * (1.0 / math.sqrt(DEVICE_ROWS * 32))
+    ad_ref[...] = total * (1.0 / math.sqrt(DEVICE_ROWS * 32))
 
     gather_drain(ix_copy)
 
@@ -669,8 +745,14 @@
         for step in range(1, 8):
             q_copy(k, step).wait_send()
         a_copy(k).wait_send()
-        for step in range(1, ZS):
-            b_copy(k, step).wait_send()
+        for zz in range(ZS):
+            @pl.when(z < zz)
+            def _():
+                b_copy(0, k, zz).wait_send()
+
+            @pl.when(z > zz)
+            def _():
+                b_copy(1, k, zz).wait_send()
 
         @pl.when(k != a)
         def _():
@@ -687,13 +769,13 @@
     vmem = pl.BlockSpec(memory_space=pltpu.VMEM)
     smem = pl.BlockSpec(memory_space=pltpu.SMEM)
     dma = pltpu.SemaphoreType.DMA
-    return pl.pallas_call(
+    dq, dk, dv, ad = pl.pallas_call(
         line_kernel,
         out_shape=(
             jax.ShapeDtypeStruct((DEVICE_ROWS, QUERY_HEADS * HEAD_SIZE), BF16),
             jax.ShapeDtypeStruct((DEVICE_ROWS, KVH * HEAD_SIZE), BF16),
             jax.ShapeDtypeStruct((DEVICE_ROWS, KVH * HEAD_SIZE), BF16),
-            jax.ShapeDtypeStruct((HEAD_SIZE, ADAPTER_RANK), F32),
+            jax.ShapeDtypeStruct((ADAPTER_RANK, HEAD_SIZE), F32),
         ),
         in_specs=[vmem] * 8 + [smem],
         out_specs=[vmem] * 4,
@@ -701,13 +783,15 @@
             pltpu.VMEM((8, KVH, 128, 256), BF16),
             pltpu.VMEM((8, 16, 128), BF16),
             pltpu.VMEM((1024, 1024), BF16),
-            pltpu.VMEM((1024, 256), F32),
+            pltpu.VMEM((512, 256), F32),
+            pltpu.VMEM((128, 256), F32),
+            pltpu.VMEM((128, 256), BF16),
             pltpu.VMEM((8 * PAIR_ROWS, 256), BF16),
             pltpu.VMEM((256, 8 * PAIR_ROWS), BF16),
-            pltpu.VMEM((1024, 1024), BF16),
-            pltpu.VMEM((1024, 1024), BF16),
-            pltpu.VMEM((1024, 128), BF16),
-            pltpu.VMEM((1024, 128), BF16),
+            pltpu.VMEM((512, 1024), BF16),
+            pltpu.VMEM((512, 1024), BF16),
+            pltpu.VMEM((1024, 256), BF16),
+            pltpu.VMEM((1024, 256), BF16),
             pltpu.VMEM((256, 256), BF16),
             pltpu.VMEM((SHORT_DEV, 256), F32),
             pltpu.VMEM((ADAPTER_RANK, 128), BF16),
@@ -715,8 +799,9 @@
             pltpu.VMEM((KVH, 8, PAIR_ROWS, 512), BF16),
             pltpu.VMEM((KVH, 2, ZS, 128, 256), BF16),
             pltpu.VMEM((KVH, ZS, 128, 256), BF16),
-            pltpu.VMEM((KVH, ZS, 128, 256), BF16),
-            pltpu.VMEM((KVH, ZS, 128, 256), BF16),
+            pltpu.VMEM((2, KVH, ZS, 128, 256), BF16),
+            pltpu.VMEM((2, KVH, ZS, 128, 256), BF16),
+            pltpu.VMEM((128, 256), F32),
             pltpu.VMEM((KVH, GROUP, ADAPTER_RANK, HEAD_SIZE), F32),
             pltpu.VMEM((4, GROUP, ADAPTER_RANK, HEAD_SIZE), F32),
             pltpu.VMEM((8, ADAPTER_RANK, HEAD_SIZE), BF16),
@@ -725,7 +810,7 @@
             dma((3, 8)), dma((8,)),
             dma((KVH, 8)), dma((KVH, 8)),
             dma((KVH,)), dma((KVH,)),
-            dma((KVH, ZS)), dma((KVH, ZS)),
+            dma((2, KVH, ZS)), dma((2, KVH, ZS)),
             dma((4,)), dma((4,)),
             dma((8,)), dma((8,)),
         ],
@@ -733,7 +818,8 @@
             collective_id=0, has_side_effects=True, vmem_limit_bytes=56 * 1024 * 1024
         ),
         cost_estimate=pl.CostEstimate(flops=10 ** 10, bytes_accessed=8 * 10 ** 6, transcendentals=4 * 10 ** 6),
-    )(q, k, v, d, og, down, own, slot, lengths)
+    )(q, k, v, d, og.T, down.T, own, slot, lengths)
+    return dq, dk, dv, ad.T
 
 
 def solution(mesh):

time: 109 us -> 106 us (0.972)
  local copies, waits for them, and re-layouts: 9.1 us -> 4.49 us
    unnamed x9 -> x10, local copies, waits for them, and re-layouts: 7.58 us -> 4.49 us
    pallas_call x1 -> x0, local copies, waits for them, and re-layouts: 1.52 us -> none  [line_shards(): pl.pallas_call(line_kernel, out_shape=(jax.ShapeDtypeStruct((DEVICE_ROWS,...]
where the time goes in v1:
time: 106 us; the launch traced here: 105 us
  Pallas kernels  100 us (94%)
  local copies, waits for them, and re-layouts  4.49 us (4%)
    pallas_call x1, Pallas kernels, line_shards(): pl.pallas_call(line_kernel, out_shape=(jax.ShapeDtypeStruct((DEVICE_ROWS,...  100 us
    unnamed x10, local copies, waits for them, and re-layouts  4.49 us

profile of v1, /device:TPU:0, one launch (start us, length us, event | category | flops | bytes accessed | tf_op | source)
XLA Modules:
  0.0 105.4 jit_solution(7849013953838142271)
XLA Ops:
  0.6 100.3 %shard_map.120 = (bf16[160,4096]{1,0:T(8,128)(2,1)}, bf16[160,512]{1,0:T(8,128)(2,1)}, bf16[160,512]{1,0:T(8,128)(2,1)}, f32[32,128]{1,0:T(8,128)}) custom-call(bf16[160,4096]{1,0:T(8,128)(2,1)} %q_ref.1, bf16[160,512]{1,0:T(8,128)(2,1)} %k_ref.1, bf16[160,512]{1,0:T(8,128)(2,1)} %v_ref.1, bf16[160,4096]{1,0:T(8,128)(2,1)} %d_ref.1, ...), custom_call_target="tpu_custom_call" | custom-call | flops 10000000000 | bytes 8000000 | tf_op jit(solution)/shard_map/pallas_call | solution.py:772
  100.9 0.0 copy-start.1
  100.9 0.0 copy-start
  100.9 0.0 copy-start.2
  101.0 2.5 %copy.17 = bf16[160,4096]{1,0:T(8,128)(2,1)} copy(bf16[160,4096]{1,0:T(8,128)(2,1)} %get-tuple-element.16) | data formatting | bytes 2621440
  103.5 0.0 copy-done.1
  103.5 0.7 copy.18
  104.2 0.0 copy-done
  104.2 0.7 copy.19
  104.8 0.0 copy-done.2
  104.8 0.6 copy.20
Async XLA Ops:
  100.9 2.6 %copy-start.1 = (bf16[160,512]{1,0:T(8,128)(2,1)S(1)}, bf16[160,512]{1,0:T(8,128)(2,1)}, u32[]{:S(2)}) copy-start(bf16[160,512]{1,0:T(8,128)(2,1)} %get-tuple-element.17) | copy-start | bytes 491524
  100.9 3.2 %copy-start = (bf16[160,512]{1,0:T(8,128)(2,1)S(1)}, bf16[160,512]{1,0:T(8,128)(2,1)}, u32[]{:S(2)}) copy-start(bf16[160,512]{1,0:T(8,128)(2,1)} %get-tuple-element.18) | copy-start | bytes 491524
  100.9 3.9 %copy-start.2 = (f32[32,128]{1,0:T(8,128)S(1)}, f32[32,128]{1,0:T(8,128)}, u32[]{:S(2)}) copy-start(f32[32,128]{1,0:T(8,128)} %get-tuple-element.11) | copy-start | bytes 49156

commit v2 on v1

--- a/solution.py
+++ b/solution.py
@@ -324,9 +324,9 @@
 
 
 def line_kernel(
-    q_ref, k_ref, v_ref, d_ref, og_ref, down_ref, own_ref, slot_ref, len_ref,
+    q_hbm, k_ref, v_ref, d_hbm, og_ref, down_ref, own_ref, slot_ref, len_ref,
     dq_ref, dk_ref, dv_ref, ad_ref,
-    kvb, idxb, perm, bias2, in_second, row_half, pack2, unpack2, w_all, ds_all, q_all, g_all, ogs_bd, bias_s,
+    q_ref, d_ref, in_sem, kvb, idxb, perm, bias2, in_second, row_half, pack2, unpack2, w_all, ds_all, q_all, g_all, ogs_bd, bias_s,
     og_t, packed, recv_q, part, recv_a, send_b, recv_b, b_total, ad_part, recv_ad, ad_sum, recv_ad2,
     ag_send, ag_recv, ix_send, ix_recv, q_send, q_recv, a_send, a_recv, b_send, b_recv,
     ad_send, ad_recv, ad2_send, ad2_recv,
@@ -342,6 +342,11 @@
             src_ref=src, dst_ref=dst, send_sem=ssem, recv_sem=rsem,
             device_id=(dp, ctx), device_id_type=MESH_ID,
         )
+
+    load_q = pltpu.make_async_copy(q_hbm, q_ref, in_sem.at[0])
+    load_d = pltpu.make_async_copy(d_hbm, d_ref, in_sem.at[1])
+    load_q.start()
+    load_d.start()
 
     barrier = pltpu.get_barrier_semaphore()
     for step in range(1, 8):
@@ -484,12 +489,14 @@
         dv_ref[short_rows, head_cols(k)] = nn(w, gs).astype(BF16)
         ad_part[k] = nt(ogs_bd[...], att_t).reshape(GROUP, ADAPTER_RANK, HEAD_SIZE)
 
+    load_q.wait()
+    load_d.wait()
     short_group(0)
     for hop in range(1, ZS):
         gather_hop(ix_copy, hop)
         gather_hop(kv_chunk(0), hop)
+        gather_steps(kv_chunk(hop))
         short_group(hop)
-    gather_steps(kv_chunk(1))
     gather_end(ix_copy)
 
     idx = idxb[...].astype(F32)
@@ -546,13 +553,26 @@
             send_b.at[way, k, zz], recv_b.at[way, k, zz], b_send.at[way, k, zz], b_recv.at[way, k, zz], a, mate
         )
 
-    def q_copy(k, step):
+    far_first = (4, 3, 5, 2, 6, 1, 7)
+
+    def q_copy(k, part_no, step):
         to = lax.rem(c + step, 8)
-        return sender(packed.at[k, to], recv_q.at[k, c], q_send.at[k, to], q_recv.at[k, c], a, to)
-
-    def q_landed(k, step):
+        return sender(
+            packed.at[k, part_no, to], recv_q.at[k, part_no, c],
+            q_send.at[k, part_no, to], q_recv.at[k, part_no, c], a, to,
+        )
+
+    def q_landed(k, part_no, step):
         frm = lax.rem(c + step, 8)
-        return sender(packed.at[k, frm], recv_q.at[k, frm], q_send.at[k, frm], q_recv.at[k, frm], a, frm)
+        return sender(
+            packed.at[k, part_no, frm], recv_q.at[k, part_no, frm],
+            q_send.at[k, part_no, frm], q_recv.at[k, part_no, frm], a, frm,
+        )
+
+    def relay(k, part_no):
+        for step in far_first:
+            q_copy(k, part_no, step).start()
+        recv_q[k, part_no, c] = packed[k, part_no, c]
 
     def ad_copy(k):
         return sender(ad_part.at[k], recv_ad.at[a], ad_send.at[k], ad_recv.at[a], k, c)
@@ -569,13 +589,32 @@
         frm = lax.rem(c + step, 8)
         return sender(ad_sum.at[frm], recv_ad2.at[frm], ad2_send.at[frm], ad2_recv.at[frm], a, frm)
 
-    def chip_sum(k):
+    last = KVH - 1
+
+    def direct(step):
+        to = lax.rem(z + step, ZS)
+        return sender(
+            part.at[last, core, to], recv_b.at[0, last, z],
+            b_send.at[0, last, to], b_recv.at[0, last, z], a, 2 * to + core,
+        )
+
+    def direct_landed(step):
+        frm = lax.rem(z + step, ZS)
+        return sender(
+            part.at[last, core, frm], recv_b.at[0, last, frm],
+            b_send.at[0, last, frm], b_recv.at[0, last, frm], a, 2 * frm + core,
+        )
+
+    def two_cores(k):
         a_copy(k).wait_recv()
         part[k, core] = (part[k, core].astype(F32) + recv_a[k].astype(F32)).astype(BF16)
 
+    def chip_sum(k):
+        two_cores(k)
+
         @pl.when(z == 0)
         def _():
-            for zz in range(1, ZS):
+            for zz in range(ZS - 1, 0, -1):
                 send_b[0, k, zz] = part[k, core, zz]
                 b_copy(0, k, zz).start()
 
@@ -593,7 +632,7 @@
 
         @pl.when(z == hop)
         def _():
-            for zz in range(hop + 1, ZS):
+            for zz in range(ZS - 1, hop, -1):
                 pass_on(0, zz)
 
         @pl.when(z == ZS - 1 - hop)
@@ -633,27 +672,33 @@
             q_all[cols, :] = qp
             g_all[cols, :] = gp
             dq_t = pick(nn(key_t, ds)).astype(BF16)
-            packed[k, :, :, p * 128:(p + 1) * 128] = (
+            packed[k, p // 2, :, :, (p % 2) * 128:(p % 2 + 1) * 128] = (
                 nt(pack2[...], dq_t).astype(BF16).reshape(8, PAIR_ROWS, HEAD_SIZE)
             )
             for h in range(2):
                 ad_part[k, 2 * p + h] += nt(og_t[...], att_t[:, h * 128:(h + 1) * 128])
 
-            @pl.when(k < KVH - 1)
+            if p == 1:
+                relay(k, 0)
+            @pl.when(k == 0)
             def _(p=p):
-                if p == 0:
-                    @pl.when(k < KVH - 2)
-                    def _():
-                        gather_steps(kv_chunk(k + 2))
-                else:
-                    gather_hop(kv_chunk(k + 1), p)
-
-            @pl.when(k > 0)
-            def _(p=p):
-                if p == 0:
+                for chunk in range(1, KVH):
+                    if 1 <= p + 3 - chunk <= 3:
+                        gather_hop(kv_chunk(chunk), p + 3 - chunk)
+
+            if p == 0:
+                @pl.when(k > 1)
+                def _():
+                    line_sum(k - 2, 2)
+
+                @pl.when(k > 0)
+                def _():
                     chip_sum(k - 1)
-                else:
-                    line_sum(k - 1, p)
+
+            if p == 2:
+                @pl.when(k > 0)
+                def _():
+                    line_sum(k - 1, 1)
 
         dk = nn(ds_all[...], q_all[...]).astype(BF16)
         dv = nn(w_all[...], g_all[...]).astype(BF16)
@@ -665,17 +710,24 @@
                 part[k, cc, zz, :, 0:128] = dk[rows, cols]
                 part[k, cc, zz, :, 128:256] = dv[rows, cols]
         a_copy(k).start()
-        for step in range(1, 8):
-            q_copy(k, step).start()
-        recv_q[k, c] = packed[k, c]
 
         @pl.when(k != a)
         def _():
             ad_copy(k).start()
 
+        @pl.when(k < KVH - 1)
+        def _():
+            relay(k, 1)
+
         return carry
 
+    gather_hop(kv_chunk(1), 1)
     lax.fori_loop(0, KVH, group, 0)
+    line_sum(KVH - 2, 2)
+    two_cores(last)
+    for step in (2, 1, 3):
+        direct(step).start()
+    relay(last, 1)
 
     me_f = c.astype(F32) * 128.0
     local = iota((128, 128), 0).astype(F32) + me_f
@@ -689,8 +741,6 @@
         holds = (from_lane & (within_f - float(SLOT_ROWS * h) == rank_line[None])).astype(F32)
         holds = holds.reshape(8 * PAIR_ROWS, 1024).astype(BF16)
         unpack2[h * 128:(h + 1) * 128, :] = nt(lands, holds).astype(BF16)
-
-    chip_sum(KVH - 1)
 
     for step in range(1, 4):
         ad_landed(step).wait_recv()
@@ -701,29 +751,34 @@
         ad2_copy(step).start()
     recv_ad2[c] = ad_sum[c]
 
-    for hop in range(1, ZS):
-        line_sum(KVH - 1, hop)
 
     def finish(k, carry):
-        for step in range(1, 8):
-            q_landed(k, step).wait_recv()
-        rows = nn(unpack2[...], recv_q[k].reshape(8 * PAIR_ROWS, 512)).astype(BF16)
-        for p in range(4):
-            for h in range(2):
-                dq_ref[long_rows, head_cols(k * GROUP + 2 * p + h)] = rows[
-                    h * 128:(h + 1) * 128, p * 128:(p + 1) * 128
-                ]
+        for part_no in range(2):
+            for step in range(1, 8):
+                q_landed(k, part_no, step).wait_recv()
+            rows = nn(unpack2[...], recv_q[k, part_no].reshape(8 * PAIR_ROWS, 256)).astype(BF16)
+            for p in range(2):
+                for h in range(2):
+                    dq_ref[long_rows, head_cols(k * GROUP + 4 * part_no + 2 * p + h)] = rows[
+                        h * 128:(h + 1) * 128, p * 128:(p + 1) * 128
+                    ]
         b_total[...] = part[k, core, z].astype(F32)
 
-        @pl.when(z > 0)
+        @pl.when((z > 0) & (k < last))
         def _():
             b_landed(0, k, z).wait_recv()
             b_total[...] += recv_b[0, k, z].astype(F32)
 
-        @pl.when(z < ZS - 1)
+        @pl.when((z < ZS - 1) & (k < last))
         def _():
             b_landed(1, k, z).wait_recv()
             b_total[...] += recv_b[1, k, z].astype(F32)
+
+        @pl.when(k == last)
+        def _():
+            for step in range(1, ZS):
+                direct_landed(step).wait_recv()
+                b_total[...] += recv_b[0, last, lax.rem(z + step, ZS)].astype(F32)
 
         dk_ref[long_rows, head_cols(k)] = b_total[:, 0:128].astype(BF16)
         dv_ref[long_rows, head_cols(k)] = b_total[:, 128:256].astype(BF16)
@@ -742,15 +797,16 @@
 
     def drain(k, carry):
         gather_drain(lambda way, s: kv_copy(way, s, k))
-        for step in range(1, 8):
-            q_copy(k, step).wait_send()
+        for part_no in range(2):
+            for step in range(1, 8):
+                q_copy(k, part_no, step).wait_send()
         a_copy(k).wait_send()
         for zz in range(ZS):
-            @pl.when(z < zz)
+            @pl.when((z < zz) & (k < last))
             def _():
                 b_copy(0, k, zz).wait_send()
 
-            @pl.when(z > zz)
+            @pl.when((z > zz) & (k < last))
             def _():
                 b_copy(1, k, zz).wait_send()
 
@@ -761,12 +817,15 @@
         return carry
 
     lax.fori_loop(0, KVH, drain, 0)
+    for step in range(1, ZS):
+        direct(step).wait_send()
     for step in range(1, 8):
         ad2_copy(step).wait_send()
 
 
 def line_shards(q, k, v, d, og, down, own, slot, lengths):
     vmem = pl.BlockSpec(memory_space=pltpu.VMEM)
+    hbm = pl.BlockSpec(memory_space=pl.ANY)
     smem = pl.BlockSpec(memory_space=pltpu.SMEM)
     dma = pltpu.SemaphoreType.DMA
     dq, dk, dv, ad = pl.pallas_call(
@@ -777,9 +836,12 @@
             jax.ShapeDtypeStruct((DEVICE_ROWS, KVH * HEAD_SIZE), BF16),
             jax.ShapeDtypeStruct((ADAPTER_RANK, HEAD_SIZE), F32),
         ),
-        in_specs=[vmem] * 8 + [smem],
+        in_specs=[hbm, vmem, vmem, hbm] + [vmem] * 4 + [smem],
         out_specs=[vmem] * 4,
         scratch_shapes=[
+            pltpu.VMEM((DEVICE_ROWS, QUERY_HEADS * HEAD_SIZE), BF16),
+            pltpu.VMEM((DEVICE_ROWS, QUERY_HEADS * HEAD_SIZE), BF16),
+            dma((2,)),
             pltpu.VMEM((8, KVH, 128, 256), BF16),
             pltpu.VMEM((8, 16, 128), BF16),
             pltpu.VMEM((1024, 1024), BF16),
@@ -795,8 +857,8 @@
             pltpu.VMEM((256, 256), BF16),
             pltpu.VMEM((SHORT_DEV, 256), F32),
             pltpu.VMEM((ADAPTER_RANK, 128), BF16),
-            pltpu.VMEM((KVH, 8, PAIR_ROWS, 512), BF16),
-            pltpu.VMEM((KVH, 8, PAIR_ROWS, 512), BF16),
+            pltpu.VMEM((KVH, 2, 8, PAIR_ROWS, 256), BF16),
+            pltpu.VMEM((KVH, 2, 8, PAIR_ROWS, 256), BF16),
             pltpu.VMEM((KVH, 2, ZS, 128, 256), BF16),
             pltpu.VMEM((KVH, ZS, 128, 256), BF16),
             pltpu.VMEM((2, KVH, ZS, 128, 256), BF16),
@@ -808,7 +870,7 @@
             pltpu.VMEM((8, ADAPTER_RANK, HEAD_SIZE), BF16),
             dma((3, 8, KVH)), dma((8, KVH)),
             dma((3, 8)), dma((8,)),
-            dma((KVH, 8)), dma((KVH, 8)),
+            dma((KVH, 2, 8)), dma((KVH, 2, 8)),
             dma((KVH,)), dma((KVH,)),
             dma((2, KVH, ZS)), dma((2, KVH, ZS)),
             dma((4,)), dma((4,)),

time: 106 us -> 88.8 us (0.84)
  Pallas kernels: 100 us -> 83.5 us
    pallas_call x1, Pallas kernels: 100 us -> 83.5 us  [line_shards(): pl.pallas_call(line_kernel, out_shape=(jax.ShapeDtypeStruct((DEVICE_ROWS,...]
where the time goes in v2:
time: 88.8 us; the launch traced here: 88.7 us
  Pallas kernels  83.5 us (94%)
  local copies, waits for them, and re-layouts  4.49 us (5%)
    pallas_call x1, Pallas kernels, line_shards(): pl.pallas_call(line_kernel, out_shape=(jax.ShapeDtypeStruct((DEVICE_ROWS,...  83.5 us
    unnamed x10, local copies, waits for them, and re-layouts  4.49 us

profile of v2, /device:TPU:0, one launch (start us, length us, event | category | flops | bytes accessed | tf_op | source)
XLA Modules:
  0.0 88.7 jit_solution(2555846206507221067)
XLA Ops:
  0.6 83.5 %shard_map.120 = (bf16[160,4096]{1,0:T(8,128)(2,1)}, bf16[160,512]{1,0:T(8,128)(2,1)}, bf16[160,512]{1,0:T(8,128)(2,1)}, f32[32,128]{1,0:T(8,128)}) custom-call(bf16[160,4096]{1,0:T(8,128)(2,1)} %q_hbm.1, bf16[160,512]{1,0:T(8,128)(2,1)} %k_ref.1, bf16[160,512]{1,0:T(8,128)(2,1)} %v_ref.1, bf16[160,4096]{1,0:T(8,128)(2,1)} %d_hbm.1, ...), custom_call_target="tpu_custom_call" | custom-call | flops 10000000000 | bytes 8000000 | tf_op jit(solution)/shard_map/pallas_call | solution.py:831
  84.1 0.0 copy-start.1
  84.2 0.0 copy-start
  84.2 0.0 copy-start.2
  84.2 2.5 %copy.17 = bf16[160,4096]{1,0:T(8,128)(2,1)} copy(bf16[160,4096]{1,0:T(8,128)(2,1)} %get-tuple-element.16) | data formatting | bytes 2621440
  86.7 0.0 copy-done.1
  86.7 0.7 copy.18
  87.4 0.0 copy-done
  87.4 0.7 copy.19
  88.0 0.0 copy-done.2
  88.1 0.6 copy.20
Async XLA Ops:
  84.1 2.6 %copy-start.1 = (bf16[160,512]{1,0:T(8,128)(2,1)S(1)}, bf16[160,512]{1,0:T(8,128)(2,1)}, u32[]{:S(2)}) copy-start(bf16[160,512]{1,0:T(8,128)(2,1)} %get-tuple-element.17) | copy-start | bytes 491524
  84.2 3.2 %copy-start = (bf16[160,512]{1,0:T(8,128)(2,1)S(1)}, bf16[160,512]{1,0:T(8,128)(2,1)}, u32[]{:S(2)}) copy-start(bf16[160,512]{1,0:T(8,128)(2,1)} %get-tuple-element.18) | copy-start | bytes 491524
  84.2 3.9 %copy-start.2 = (f32[32,128]{1,0:T(8,128)S(1)}, f32[32,128]{1,0:T(8,128)}, u32[]{:S(2)}) copy-start(f32[32,128]{1,0:T(8,128)} %get-tuple-element.11) | copy-start | bytes 49156
